TPU v7x, 32 devices: a whole 2x2x4 slice. The times are simulated.
32 devices in a mesh: groups: 2 (over x), tok: 16 (over z, y, core).
Axes of the slice: x: 2, y: 2, z: 4, core: 2. Of those that a mesh axis runs over, the one named last changes fastest.
Arguments:
- queries: bfloat16 [2, 8192, 1024], P(None, ('groups', 'tok')), parts along dimension 1, may hold values from -6 to 6
- keys: bfloat16 [2, 8192, 1024], P(None, ('groups', 'tok')), parts along dimension 1, may hold values from -6 to 6
- values: bfloat16 [2, 8192, 1024], P(None, ('groups', 'tok')), parts along dimension 1, may hold values from -6 to 6
- rates: float32 [2, 3, 2, 8192], P(None, None, None, ('groups', 'tok')), parts along dimension 3, may hold values from 0.0002 to 0.002
- fast_weights: float32 [2, 3, 512, 512], P(None, None, 'tok'), may hold values from -0.25 to 0.25
Outputs:
- attended: bfloat16 [2, 8192, 1024], P(None, ('groups', 'tok')), parts along dimension 1
- final_weights: float32 [4, 3, 512, 512], P('groups', None, 'tok'), parts along dimension 0
There are 2 independent parts, one for each index of `groups`. A program takes and returns all parts, laid end to end along the dimension named above; an argument that names none is the same for every part. Nothing has to cross between parts.
All inputs are finite; a program needn't handle non-finite values.
Results may differ from a plain program's by a relative error of at most 0.0098.
Values may be sent and summed in bfloat16 or wider, within the bound.
A program may use at most 64 MiB of HBM per device.

v0:
```python
import jax
import jax.numpy as jnp
from jax import lax
from jax.sharding import PartitionSpec as P


def cross(left, right):
    return lax.dot_general(
        left, right, (((1,), (1,)), ((), ())), preferred_element_type=jnp.float32
    )


def inner(left, right):
    return lax.dot_general(
        left, right, (((0,), (0,)), ((), ())), preferred_element_type=jnp.float32
    )


def renorm(old, upd):
    old_norm = jnp.sqrt(jnp.mean(old * old, axis=-1))
    new_norm = jnp.sqrt(jnp.mean(upd * upd, axis=-1) + 1e-06)
    return upd * (old_norm / new_norm)[..., None]


def head_step(query, key_rows, value_rows, rate_rows, wbf):
    hidden_q = (jax.nn.silu(cross(query, wbf[0])) * cross(query, wbf[1])).astype(jnp.bfloat16)
    raw = cross(hidden_q, wbf[2])
    normed = (raw / jnp.sqrt(jnp.mean(raw * raw, axis=-1, keepdims=True) + 1e-06)).astype(
        jnp.bfloat16
    )
    h1 = cross(key_rows, wbf[0])
    h3 = cross(key_rows, wbf[1])
    sig = jax.nn.sigmoid(h1)
    act = h1 * sig
    back = jnp.dot(value_rows, wbf[2], preferred_element_type=jnp.float32)
    d1 = back * h3 * sig * (1.0 + h1 * (1.0 - sig))
    d3 = back * act
    e1 = (rate_rows[0][:, None] * d1).astype(jnp.bfloat16)
    e3 = (rate_rows[1][:, None] * d3).astype(jnp.bfloat16)
    b2 = (rate_rows[2][:, None] * (act * h3)).astype(jnp.bfloat16)
    grad = jnp.stack([inner(e1, key_rows), inner(e3, key_rows), inner(value_rows, b2)])
    return (normed, grad)


def block_step(span, gathered, queries, keys, values, rates):
    heads = gathered.shape[0]
    width = gathered.shape[3]
    pieces = []
    grads = []
    for head in range(heads):
        lo = head * width
        normed, grad = head_step(
            queries[span][:, lo : lo + width],
            keys[span][:, lo : lo + width],
            values[span][:, lo : lo + width],
            rates[span][:, head],
            gathered[head],
        )
        pieces.append(normed)
        grads.append(grad)
    return (jnp.concatenate(pieces, axis=1), jnp.stack(grads))


def fetch(own):
    return lax.all_gather(own.astype(jnp.bfloat16), "tok", axis=2, tiled=True)


def settle(partial_value, own):
    total = lax.psum_scatter(partial_value, "tok", scatter_dimension=2, tiled=True)
    return renorm(own, own + total)


def on_device(queries, keys, values, rates, fast_weights):
    nblocks = queries.shape[0]
    own = fast_weights
    blocks = []
    for span in range(nblocks):
        gathered = fetch(own)
        normed, partial_value = block_step(span, gathered, queries, keys, values, rates)
        blocks.append(normed)
        own = settle(partial_value, own)
    return (jnp.stack(blocks), own)


def solution(mesh):
    placed = (
        P(None, ("groups", "tok"), None),
        P(None, ("groups", "tok"), None),
        P(None, ("groups", "tok"), None),
        P(None, None, None, ("groups", "tok")),
        P(None, None, "tok", None),
    )
    return jax.shard_map(
        on_device,
        mesh=mesh,
        in_specs=placed,
        out_specs=(P(None, ("groups", "tok"), None), P("groups", None, "tok", None)),
        check_vma=False,
    )
```

profile of v0, /device:TPU:0, one launch (start us, length us, event | category | flops | bytes accessed | tf_op | source)
XLA Modules:
  0.0 309.0 jit_solution(13420339890189697955)
XLA Ops:
  7.2 1.9 multiply_reduce_fusion.7
  10.5 2.2 slice_bitcast_fusion.12
  12.8 1.1 slice_bitcast_fusion.13
  13.8 44.9 %all-gather.3.cloned.1.call-done = bf16[2,3,512,512]{3,2,1,0:T(8,128)(2,1)} async-done(((bf16[2,3,32,512]{3,2,1,0:T(8,128)(2,1)}), bf16[2,3,512,512]{3,2,1,0:T(8,128)(2,1)}) %all-gather.3.cloned.1.call-update) | async-done | bytes 3145744 | tf_op jit(solution)/shard_map/all_gather | solution.py:65
  58.7 1.6 fusion.34
  60.3 1.4 fusion.37
  61.7 1.4 convolution_bitcast_fusion.10
  67.7 3.4 %pad_maximum_fusion = f32[2,3,512,512]{3,2,1,0:T(8,128)} fusion(f32[1,3,512,512]{3,2,1,0:T(8,128)S(1)} %maximum_bitcast_fusion.1, f32[1,3,512,512]{3,2,1,0:T(8,128)S(1)} %maximum_bitcast_fusion), kind=kLoop, calls=%fused_computation | loop fusion | flops 1572864 | bytes 12582912 | tf_op jit(solution)/shard_map/stack | solution.py:61
  71.2 84.1 %reduce-scatter.3.cloned.1.call-done = f32[2,3,32,512]{3,2,1,0:T(8,128)} async-done(((f32[2,3,512,512]{3,2,1,0:T(8,128)}), f32[2,3,32,512]{3,2,1,0:T(8,128)}) %reduce-scatter.3.cloned.1.call-update) | async-done | bytes 393232 | tf_op jit(solution)/shard_map/reduce_scatter | solution.py:69
  155.3 1.2 multiply_reduce_fusion.6
  157.6 45.2 %all-gather.5.cloned.1.call-done = bf16[2,3,512,512]{3,2,1,0:T(8,128)(2,1)} async-done(((bf16[2,3,32,512]{3,2,1,0:T(8,128)(2,1)}), bf16[2,3,512,512]{3,2,1,0:T(8,128)(2,1)}) %all-gather.5.cloned.1.call-update) | async-done | bytes 3145744 | tf_op jit(solution)/shard_map/all_gather | solution.py:65
  202.8 1.6 convolution_bitcast_fusion.16
  204.4 1.4 convolution_bitcast_fusion.13
  205.8 1.4 convolution_bitcast_fusion.4
  211.8 3.4 %pad_maximum_fusion.1 = f32[2,3,512,512]{3,2,1,0:T(8,128)} fusion(f32[1,3,512,512]{3,2,1,0:T(8,128)S(1)} %maximum_bitcast_fusion.3, f32[1,3,512,512]{3,2,1,0:T(8,128)S(1)} %maximum_bitcast_fusion.2), kind=kLoop, calls=%fused_computation.1 | loop fusion | flops 1572864 | bytes 12582912 | tf_op jit(solution)/shard_map/stack | solution.py:61
  215.2 2.1 slice_bitcast_fusion.17
  218.1 1.2 fusion.39
  219.2 2.5 multiply_reduce_fusion.2
  221.7 2.1 fusion.35
  223.8 2.6 multiply_reduce_fusion.3
  226.4 1.6 divide_convert_fusion.2
  228.0 0.9 maximum_bitcast_fusion.4
  228.8 2.3 convolution_bitcast_fusion.19
  231.1 2.6 multiply_reduce_fusion
  233.7 2.1 convolution_bitcast_fusion.21
  235.8 2.5 multiply_reduce_fusion.1
  238.3 1.1 divide_convert_fusion
  239.5 1.1 divide_convert_fusion.1
  240.7 2.1 pad_maximum_fusion.2
  242.8 56.6 %reduce-scatter.5.cloned.1.call-done = f32[2,3,32,512]{3,2,1,0:T(8,128)} async-done(((f32[2,3,512,512]{3,2,1,0:T(8,128)}), f32[2,3,32,512]{3,2,1,0:T(8,128)}) %reduce-scatter.5.cloned.1.call-update) | async-done | bytes 393232 | tf_op jit(solution)/shard_map/reduce_scatter | solution.py:69
  299.4 1.2 multiply_reduce_fusion.5
  300.6 1.9 broadcast_multiply_fusion
  (64 shorter events, 12.3 us)
Async XLA Ops:
  7.2 5.6 %copy-start.8 = (bf16[2,256,1024]{2,1,0:T(8,128)(2,1)S(1)}, bf16[2,256,1024]{2,1,0:T(8,128)(2,1)}, u32[]{:S(2)}) copy-start(bf16[2,256,1024]{2,1,0:T(8,128)(2,1)} %param.7) | copy-start | bytes 3145732
  7.2 51.5 %all-gather.3.cloned.1.call-start = ((), (), s32[]{:S(2)}) async-start(), calls=%async_computation.2 | async-start | bytes 3342336 | tf_op jit(solution)/shard_map/all_gather | solution.py:65
  9.2 146.1 %reduce-scatter.3.cloned.1.call-start = ((), (), s32[]{:S(2)}) async-start(), calls=%async_computation.3 | async-start | bytes 6684672 | tf_op jit(solution)/shard_map/reduce_scatter | solution.py:69
  58.7 4.5 %copy-start = (bf16[2,3,512,512]{3,2,1,0:T(8,128)(2,1)S(1)}, bf16[2,3,512,512]{3,2,1,0:T(8,128)(2,1)}, u32[]{:S(2)}) copy-start(bf16[2,3,512,512]{3,2,1,0:T(8,128)(2,1)} %all-gather.3.cloned.1.call-done) | copy-start | bytes 9437188
  58.7 4.5 %copy-start.4 = (bf16[256,1024]{1,0:T(8,128)(2,1)S(1)}, bf16[256,1024]{1,0:T(8,128)(2,1)}, u32[]{:S(2)}) copy-start(bf16[256,1024]{1,0:T(8,128)(2,1)} %get-tuple-element.9) | copy-start | bytes 1572868
  63.2 1.0 copy-start.6
  71.1 131.7 %all-gather.5.cloned.1.call-start = ((), (), s32[]{:S(2)}) async-start(), calls=%async_computation.4 | async-start | bytes 3342336 | tf_op jit(solution)/shard_map/all_gather | solution.py:65
  157.4 142.0 %reduce-scatter.5.cloned.1.call-start = ((), (), s32[]{:S(2)}) async-start(), calls=%async_computation.5 | async-start | bytes 6684672 | tf_op jit(solution)/shard_map/reduce_scatter | solution.py:69
  202.8 4.5 %copy-start.1 = (bf16[2,3,512,512]{3,2,1,0:T(8,128)(2,1)S(1)}, bf16[2,3,512,512]{3,2,1,0:T(8,128)(2,1)}, u32[]{:S(2)}) copy-start(bf16[2,3,512,512]{3,2,1,0:T(8,128)(2,1)} %all-gather.5.cloned.1.call-done) | copy-start | bytes 9437188
  202.8 4.5 %copy-start.3 = (bf16[256,1024]{1,0:T(8,128)(2,1)S(1)}, bf16[256,1024]{1,0:T(8,128)(2,1)}, u32[]{:S(2)}) copy-start(bf16[256,1024]{1,0:T(8,128)(2,1)} %get-tuple-element.8) | copy-start | bytes 1572868
  204.4 3.2 %copy-start.11 = (f32[1,1,256]{2,1,0:T(1,128)S(1)}, f32[1,1,256]{2,1,0:T(1,128)}, u32[]{:S(2)}) copy-start(f32[1,1,256]{2,1,0:T(1,128)} %get-tuple-element.16) | copy-start | bytes 3076
  207.3 1.0 copy-start.5
  207.3 1.0 copy-start.10
  208.2 1.3 copy-start.9
  217.3 0.8 copy-start.7
  226.4 4.7 %copy-start.2 = (bf16[2,3,512,512]{3,2,1,0:T(8,128)(2,1)S(1)}, bf16[2,3,512,512]{3,2,1,0:T(8,128)(2,1)}, u32[]{:S(2)}) copy-start(bf16[2,3,512,512]{3,2,1,0:T(8,128)(2,1)} %all-gather.5.cloned.1.call-done) | copy-start | bytes 9437188
Sparse Core Ops, SparseCore 0:
  10.8 47.9 all-gather.2
  71.2 84.0 reduce-scatter.2
  158.3 44.4 all-gather.4
  215.3 83.9 reduce-scatter.4
where the time goes:
time: 310 us; the launch traced here: 309 us
  waiting for transfers between devices  231 us (75%)
  matrix products  33.9 us (11%)
  other arithmetic  21.9 us (7%)
  between operations  14.1 us (5%)
  local copies, waits for them, and re-layouts  7.79 us (3%)
    reduce_scatter x2, waiting for transfers between devices, settle(): lax.psum_scatter(partial_value, 'tok', scatter_dimension=2, tiled=True)  141 us
    all_gather x2, waiting for transfers between devices, fetch(): return lax.all_gather(own.astype(jnp.bfloat16), 'tok', axis=2, tiled=True)  90.1 us
    dot_general x16, matrix products, cross(): lax.dot_general(left, right, (((1,), (1,)), ((), ())), preferred_element_...  22.9 us
    another operation x6, other arithmetic, block_step(): return (jnp.concatenate(pieces, axis=1), jnp.stack(grads))  7.97 us
    dot_general x12, matrix products, inner(): lax.dot_general(left, right, (((0,), (0,)), ((), ())), preferred_element_...  7.62 us
  transfers between devices with their start and end apart: 4, of which 4 were waited for; matrix products, arithmetic and copies ran while one was open for 10% of the time, Pallas kernels for 0%

commit v1 on v0

v1 whole, which is shorter than its diff:
```python
import functools
import jax
import jax.numpy as jnp
from jax import lax
from jax.experimental import pallas as pl
from jax.experimental.pallas import tpu as pltpu
from jax.sharding import PartitionSpec as P

F32 = jnp.float32
BF16 = jnp.bfloat16


def cross(left, right):
    return lax.dot_general(left, right, (((1,), (1,)), ((), ())), preferred_element_type=F32)


def inner(left, right):
    return lax.dot_general(left, right, (((0,), (0,)), ((), ())), preferred_element_type=F32)


def renorm(old, upd):
    old_norm = jnp.sqrt(jnp.mean(old * old, axis=-1, keepdims=True))
    new_norm = jnp.sqrt(jnp.mean(upd * upd, axis=-1, keepdims=True) + 1e-06)
    return upd * (old_norm / new_norm)


def head_step(query, key_rows, value_rows, rate_rows, wbf):
    hidden_q = (jax.nn.silu(cross(query, wbf[0])) * cross(query, wbf[1])).astype(BF16)
    raw = cross(hidden_q, wbf[2])
    normed = (raw / jnp.sqrt(jnp.mean(raw * raw, axis=-1, keepdims=True) + 1e-06)).astype(BF16)
    h1 = cross(key_rows, wbf[0])
    h3 = cross(key_rows, wbf[1])
    sig = jax.nn.sigmoid(h1)
    act = h1 * sig
    back = jnp.dot(value_rows, wbf[2], preferred_element_type=F32)
    d1 = back * h3 * sig * (1.0 + h1 * (1.0 - sig))
    d3 = back * act
    e1 = (rate_rows[0][:, None] * d1).astype(BF16)
    e3 = (rate_rows[1][:, None] * d3).astype(BF16)
    b2 = (rate_rows[2][:, None] * (act * h3)).astype(BF16)
    grad = jnp.stack([inner(e1, key_rows), inner(e3, key_rows), inner(value_rows, b2)])
    return (normed, grad)


def plain_on_device(queries, keys, values, rates, fast_weights):
    own = fast_weights
    heads, _, _, width = own.shape
    blocks = []
    for span in range(queries.shape[0]):
        gathered = lax.all_gather(own.astype(BF16), "tok", axis=2, tiled=True)
        pieces, grads = [], []
        for head in range(heads):
            cols = slice(head * width, (head + 1) * width)
            normed, grad = head_step(
                queries[span][:, cols],
                keys[span][:, cols],
                values[span][:, cols],
                rates[span][:, head],
                gathered[head],
            )
            pieces.append(normed)
            grads.append(grad)
        blocks.append(jnp.concatenate(pieces, axis=1))
        total = lax.psum_scatter(jnp.stack(grads), "tok", scatter_dimension=2, tiled=True)
        own = renorm(own, own + total)
    return (jnp.stack(blocks), own)


def merge(*gens):
    gens = list(gens)
    while gens:
        for gen in list(gens):
            try:
                next(gen)
            except StopIteration:
                gens.remove(gen)


def kernel(
    nz, ny,
    q_hbm, k_hbm, v_hbm, rates_ref, w_ref,
    out_ref, fin_ref,
    q_ref, k_ref, v_ref, vt_ref, cur, wg, part, sibrecv, ysend, yrecv, zsend, zrecv, acc,
    in_sem, ag_ssem, ag_rsem, sib_ssem, sib_rsem, y_ssem, y_rsem, z_ssem, z_rsem,
):
    spans, tokens, _ = q_ref.shape
    heads, _, rows, dh = w_ref.shape
    tok = 2 * nz * ny
    units = nz * ny
    hid = tok * rows

    me = lax.axis_index("tok")
    c = lax.rem(me, 2)
    y = lax.rem(me // 2, ny)
    z = me // (2 * ny)
    up = me + 2 * ny
    down = me - 2 * ny
    across = me + 2 * (1 - 2 * y)
    sib = me + 1 - 2 * c

    def at(zz, yy, cc):
        return (zz * ny + yy) * 2 + cc

    def rdma(src, dst, ssem, rsem, dev):
        return pltpu.make_async_remote_copy(
            src_ref=src, dst_ref=dst, send_sem=ssem, recv_sem=rsem,
            device_id={"tok": dev}, device_id_type=pl.DeviceIdType.MESH,
        )

    loads = [
        pltpu.make_async_copy(src, dst, in_sem.at[i])
        for i, (src, dst) in enumerate(((k_hbm, k_ref), (v_hbm, v_ref), (q_hbm, q_ref)))
    ]
    for load in loads:
        load.start()

    barrier = pltpu.get_barrier_semaphore()

    def greet(dev):
        pl.semaphore_signal(
            barrier, inc=1, device_id={"tok": dev}, device_id_type=pl.DeviceIdType.MESH
        )

    pl.when(z < nz - 1)(lambda: greet(up))
    pl.when(z > 0)(lambda: greet(down))
    if ny > 1:
        greet(across)
    greet(sib)
    for h in range(heads):
        cur[h] = w_ref[h]
        wg[0, h, me] = w_ref[h].astype(BF16)
    pl.semaphore_wait(
        barrier,
        jnp.where(z < nz - 1, 1, 0) + jnp.where(z > 0, 1, 0) + (2 if ny > 1 else 1),
    )

    def ag_copy(s, h, slot, way):
        dev = (up, down, across, sib)[way]
        ref = wg.at[s, h, slot]
        return rdma(ref, ref, ag_ssem.at[s, h, way, slot], ag_rsem.at[s, h, slot], dev)

    def ag_start(s, h):
        pl.when(z < nz - 1)(lambda: ag_copy(s, h, me, 0).start())
        pl.when(z > 0)(lambda: ag_copy(s, h, me, 1).start())
        if ny > 1:
            ag_copy(s, h, me, 2).start()
        ag_copy(s, h, me, 3).start()

    def ag_steps(s, h):
        def from_z(slot, way):
            ag_copy(s, h, slot, way).wait_recv()
            pl.when((z < nz - 1) if way == 0 else (z > 0))(
                lambda: ag_copy(s, h, slot, way).start()
            )
            if ny > 1:
                ag_copy(s, h, slot, 2).start()
            ag_copy(s, h, slot, 3).start()

        def from_y(slot):
            ag_copy(s, h, slot, 3).wait_recv()
            ag_copy(s, h, slot, 3).start()

        for j in range(1, nz + 1):
            if j < nz:
                pl.when(z - j >= 0)(lambda: from_z(at(z - j, y, c), 0))
                pl.when(z + j < nz)(lambda: from_z(at(z + j, y, c), 1))
            if ny > 1:
                d = j - 1
                if d == 0:
                    from_y(at(z, 1 - y, c))
                else:
                    pl.when(z - d >= 0)(lambda: from_y(at(z - d, 1 - y, c)))
                    pl.when(z + d < nz)(lambda: from_y(at(z + d, 1 - y, c)))
            yield
        for u in range(units):
            ag_copy(s, h, u * 2 + 1 - c, 3).wait_recv()

    def ag_drain(s, h):
        for zz in range(nz):
            slot = at(zz, y, c)
            pl.when((zz <= z) & (z < nz - 1))(lambda: ag_copy(s, h, slot, 0).wait_send())
            pl.when((zz >= z) & (z > 0))(lambda: ag_copy(s, h, slot, 1).wait_send())
            if ny > 1:
                ag_copy(s, h, slot, 2).wait_send()
            for yy in range(ny):
                ag_copy(s, h, at(zz, yy, c), 3).wait_send()

    def weight(s, h, m):
        return wg[s, h, :, m].reshape(hid, dh)

    def cols(h):
        return slice(h * dh, (h + 1) * dh)

    def sib_copy(s, h, m):
        return rdma(
            part.at[s, h, m, 1 - c], sibrecv.at[s, h, m],
            sib_ssem.at[s, h, m], sib_rsem.at[s, h, m], sib,
        )

    def give(s, h, m, grad):
        grad = grad.astype(BF16).reshape(units, 2, rows, dh)
        part[s, h, m, 0] = grad[:, 0]
        part[s, h, m, 1] = grad[:, 1]
        sib_copy(s, h, m).start()

    def kv_steps(s, h):
        key = k_ref[s, :, cols(h)]
        h1 = cross(weight(s, h, 0), key)
        h3 = cross(weight(s, h, 1), key)
        yield
        back = inner(weight(s, h, 2), vt_ref[s, h])
        sig = 1.0 / (1.0 + jnp.exp(-h1))
        act = h1 * sig
        b2 = (rates_ref[s, 2, h : h + 1, :] * (act * h3)).astype(BF16)
        give(s, h, 2, cross(vt_ref[s, h], b2))
        yield
        e1 = (
            rates_ref[s, 0, h : h + 1, :] * (back * h3 * sig * (1.0 + h1 * (1.0 - sig)))
        ).astype(BF16)
        give(s, h, 0, jnp.dot(e1, key, preferred_element_type=F32))
        yield
        e3 = (rates_ref[s, 1, h : h + 1, :] * (back * act)).astype(BF16)
        give(s, h, 1, jnp.dot(e3, key, preferred_element_type=F32))
        yield

    def q_steps(s, h):
        query = q_ref[s, :, cols(h)]
        h1 = cross(query, weight(s, h, 0))
        h3 = cross(query, weight(s, h, 1))
        hidden = (h1 / (1.0 + jnp.exp(-h1)) * h3).astype(BF16)
        yield
        raw = cross(hidden, weight(s, h, 2))
        scale = lax.rsqrt(jnp.mean(raw * raw, axis=-1, keepdims=True) + 1e-06)
        out_ref[s, :, cols(h)] = (raw * scale).astype(BF16)
        yield

    def y_copy(s, h, zd):
        return rdma(
            ysend.at[s, h, zd], yrecv.at[s, h, zd],
            y_ssem.at[s, h, zd], y_rsem.at[s, h, zd], across,
        )

    def z_copy(s, h, zd, way):
        return rdma(
            zsend.at[s, h, zd], zrecv.at[s, h, way, zd],
            z_ssem.at[s, h, zd], z_rsem.at[s, h, way, zd], (up, down)[way],
        )

    def pair(s, h, m, u):
        return part[s, h, m, c, u].astype(F32) + sibrecv[s, h, m, u].astype(F32)

    def rs_steps(s, h):
        for m in (2, 0, 1):
            sib_copy(s, h, m).wait_recv()

        def send_y(zd):
            for m in range(3):
                ysend[s, h, zd, m] = pair(s, h, m, zd * ny + 1 - y).astype(BF16)
            y_copy(s, h, zd).start()

        if ny > 1:
            for d in range(nz - 1, 0, -1):
                pl.when(z + d < nz)(lambda: send_y(z + d))
                pl.when(z - d >= 0)(lambda: send_y(z - d))
            send_y(z)
        yield

        def quad(zd, m):
            value = pair(s, h, m, zd * ny + y)
            if ny > 1:
                value = value + yrecv[s, h, zd, m].astype(F32)
            return value

        def send_z(zd, way):
            more = (z > 0) if way == 0 else (z < nz - 1)
            if ny > 1:
                y_copy(s, h, zd).wait_recv()

            @pl.when(more)
            def _():
                z_copy(s, h, zd, way).wait_recv()
                for m in range(3):
                    zsend[s, h, zd, m] = (
                        quad(zd, m) + zrecv[s, h, way, zd, m].astype(F32)
                    ).astype(BF16)

            @pl.when(jnp.logical_not(more))
            def _():
                for m in range(3):
                    zsend[s, h, zd, m] = quad(zd, m).astype(BF16)

            z_copy(s, h, zd, way).start()

        for d in range(nz - 1, 0, -1):
            pl.when(z + d < nz)(lambda: send_z(z + d, 0))
            pl.when(z - d >= 0)(lambda: send_z(z - d, 1))
            yield
        if ny > 1:
            y_copy(s, h, z).wait_recv()
        for m in range(3):
            acc[m] = quad(z, m)

        def add(way):
            z_copy(s, h, z, way).wait_recv()
            for m in range(3):
                acc[m] = acc[m] + zrecv[s, h, way, z, m].astype(F32)

        pl.when(z > 0)(lambda: add(0))
        pl.when(z < nz - 1)(lambda: add(1))
        old = cur[h]
        new = renorm(old, old + acc[...])
        if s + 1 < spans:
            cur[h] = new
            wg[s + 1, h, me] = new.astype(BF16)
            ag_start(s + 1, h)
        else:
            fin_ref[h] = new

    def rs_drain(s, h):
        for m in range(3):
            sib_copy(s, h, m).wait_send()
        for zd in range(nz):
            if ny > 1:
                y_copy(s, h, zd).wait_send()
            pl.when(zd > z)(lambda: z_copy(s, h, zd, 0).wait_send())
            pl.when(zd < z)(lambda: z_copy(s, h, zd, 1).wait_send())

    def then(*gens):
        for gen in gens:
            yield from gen

    for h in range(heads):
        ag_start(0, h)
    loads[0].wait()
    loads[1].wait()
    for s in range(spans):
        for h in range(heads):
            vt_ref[s, h] = v_ref[s, :, cols(h)].T
    loads[2].wait()

    for s in range(spans):
        if s == 0:
            merge(ag_steps(s, 0))
        for h in range(heads):
            others = []
            if h + 1 < heads:
                others.append(ag_steps(s, h + 1))
            if h > 0:
                others.append(rs_steps(s, h - 1))
            merge(kv_steps(s, h), *others)
        last = [rs_steps(s, heads - 1)]
        if s + 1 < spans:
            last.append(ag_steps(s + 1, 0))
        merge(then(*[q_steps(s, h) for h in range(heads)]), *last)
    for s in range(spans):
        for h in range(heads):
            ag_drain(s, h)
            rs_drain(s, h)


def fused_on_device(nz, ny, queries, keys, values, rates, fast_weights):
    spans, tokens, width = queries.shape
    heads, three, rows, dh = fast_weights.shape
    tok = 2 * nz * ny
    units = nz * ny
    unit = (three, rows, dh)
    sh = (spans, heads)
    vmem = pl.BlockSpec(memory_space=pltpu.VMEM)
    hbm = pl.BlockSpec(memory_space=pl.ANY)
    dma = pltpu.SemaphoreType.DMA
    flops = 18 * spans * heads * tokens * dh * tok * rows
    return pl.pallas_call(
        functools.partial(kernel, nz, ny),
        out_shape=(
            jax.ShapeDtypeStruct(queries.shape, BF16),
            jax.ShapeDtypeStruct(fast_weights.shape, F32),
        ),
        in_specs=[hbm, hbm, hbm, vmem, vmem],
        out_specs=(vmem, vmem),
        scratch_shapes=[
            pltpu.VMEM(queries.shape, BF16),
            pltpu.VMEM(queries.shape, BF16),
            pltpu.VMEM(queries.shape, BF16),
            pltpu.VMEM(sh + (dh, tokens), BF16),
            pltpu.VMEM(fast_weights.shape, F32),
            pltpu.VMEM(sh + (tok,) + unit, BF16),
            pltpu.VMEM(sh + (three, 2, units, rows, dh), BF16),
            pltpu.VMEM(sh + (three, units, rows, dh), BF16),
            pltpu.VMEM(sh + (nz,) + unit, BF16),
            pltpu.VMEM(sh + (nz,) + unit, BF16),
            pltpu.VMEM(sh + (nz,) + unit, BF16),
            pltpu.VMEM(sh + (2, nz) + unit, BF16),
            pltpu.VMEM(unit, F32),
            dma((3,)),
            dma(sh + (4, tok)),
            dma(sh + (tok,)),
            dma(sh + (three,)),
            dma(sh + (three,)),
            dma(sh + (nz,)),
            dma(sh + (nz,)),
            dma(sh + (nz,)),
            dma(sh + (2, nz)),
        ],
        compiler_params=pltpu.CompilerParams(
            collective_id=0, has_side_effects=True, vmem_limit_bytes=56 * 1024 * 1024
        ),
        cost_estimate=pl.CostEstimate(
            flops=flops, bytes_accessed=8 * queries.size, transcendentals=0
        ),
    )(queries, keys, values, rates, fast_weights)


def solution(mesh):
    placed = (
        P(None, ("groups", "tok"), None),
        P(None, ("groups", "tok"), None),
        P(None, ("groups", "tok"), None),
        P(None, None, None, ("groups", "tok")),
        P(None, None, "tok", None),
    )
    tok = mesh.shape["tok"]

    def on_device(queries, keys, values, rates, fast_weights):
        rows = fast_weights.shape[2]
        if rows % 16 or tok % 4:
            return plain_on_device(queries, keys, values, rates, fast_weights)
        return fused_on_device(tok // 4, 2, queries, keys, values, rates, fast_weights)

    return jax.shard_map(
        on_device,
        mesh=mesh,
        in_specs=placed,
        out_specs=(P(None, ("groups", "tok"), None), P("groups", None, "tok", None)),
        check_vma=False,
    )
```

time: 310 us -> 130 us (0.42)
  waiting for transfers between devices: 231 us -> 0 us
  Pallas kernels: 0 us -> 126 us
  matrix products: 33.9 us -> 0 us
  other arithmetic: 21.9 us -> 0 us
  between operations: 14.1 us -> 0.65 us
  local copies, waits for them, and re-layouts: 7.79 us -> 3.06 us
    reduce_scatter x2 -> x0, waiting for transfers between devices: 141 us -> none  [settle(): lax.psum_scatter(partial_value, 'tok', scatter_dimension=2, tiled=True)]
    pallas_call x0 -> x1, Pallas kernels: none -> 126 us  [fused_on_device(): pl.pallas_call(functools.partial(kernel, nz, ny), out_shape=(jax.ShapeDty...]
    all_gather x2 -> x0, waiting for transfers between devices: 90.1 us -> none  [fetch(): return lax.all_gather(own.astype(jnp.bfloat16), 'tok', axis=2, tiled=True)]
    dot_general x32 -> x0, matrix products: 33.9 us -> none  [the longest x16 22.9 us: cross(): lax.dot_general(left, right, (((1,), (1,)), ((), ())), preferred_element_...]
    another operation x9 -> x0, other arithmetic: 11 us -> none  [the longest x6 7.97 us: block_step(): return (jnp.concatenate(pieces, axis=1), jnp.stack(grads))]
    squeeze x4 -> x0, local copies, waits for them, and re-layouts: 6.06 us -> none  [the longest x1 2.23 us: block_step(): keys[span][:, lo:lo + width]]
    convert_element_type x4 -> x0, other arithmetic: 4.64 us -> none  [the longest x3 3.86 us: head_step(): (raw / jnp.sqrt(jnp.mean(raw * raw, axis=-1, keepdims=True) + 1e-06)).ast...]
    reduce_sum x3 -> x0, other arithmetic: 4.37 us -> none  [the longest x2 3.14 us: renorm(): old_norm = jnp.sqrt(jnp.mean(old * old, axis=-1))]
  transfers between devices with their start and end apart: 4 -> 0, of which waited for: 4 -> 0; matrix products, arithmetic and copies ran while one was open for 10% -> 0% of each run, Pallas kernels for 0% -> 0%
where the time goes in v1:
time: 130 us
  Pallas kernels  126 us (97%)
  local copies, waits for them, and re-layouts  3.06 us (2%)
    pallas_call x1, Pallas kernels, fused_on_device(): pl.pallas_call(functools.partial(kernel, nz, ny), out_shape=(jax.ShapeDty...  126 us
    unnamed x4, local copies, waits for them, and re-layouts  3.06 us

profile of v1, /device:TPU:0, one launch (start us, length us, event | category | flops | bytes accessed | tf_op | source)
XLA Modules:
  0.0 129.9 jit_solution(16411411461147747775)
XLA Ops:
  0.6 126.2 %shard_map.68 = (bf16[2,256,1024]{2,1,0:T(8,128)(2,1)}, f32[2,3,32,512]{3,2,1,0:T(8,128)}) custom-call(bf16[2,256,1024]{2,1,0:T(8,128)(2,1)} %q_hbm.1, bf16[2,256,1024]{2,1,0:T(8,128)(2,1)} %k_hbm.1, bf16[2,256,1024]{2,1,0:T(8,128)(2,1)} %v_hbm.1, f32[2,3,2,256]{3,2,1,0:T(2,128)} %rates_ref.1, f32[2,3,32,512]{3,2,1,0:T(8,128)} %w_ref.1), custom_call_target="tpu_custom_call" | custom-call | flops 4831838208 | bytes 4194304 | tf_op jit(solution)/shard_map/pallas_call | solution.py:372
  126.8 0.0 copy-start
  126.8 2.3 %copy.9 = bf16[2,256,1024]{2,1,0:T(8,128)(2,1)} copy(bf16[2,256,1024]{2,1,0:T(8,128)(2,1)} %get-tuple-element.4) | data formatting | bytes 2097152
  129.1 0.0 copy-done
  129.1 0.7 copy.10
Async XLA Ops:
  126.8 2.3 %copy-start = (f32[2,3,32,512]{3,2,1,0:T(8,128)S(1)}, f32[2,3,32,512]{3,2,1,0:T(8,128)}, u32[]{:S(2)}) copy-start(f32[2,3,32,512]{3,2,1,0:T(8,128)} %get-tuple-element.5) | copy-start | bytes 1179652

commit v2 on v1

--- a/solution.py
+++ b/solution.py
@@ -66,14 +66,11 @@
     return (jnp.stack(blocks), own)
 
 
-def merge(*gens):
-    gens = list(gens)
-    while gens:
-        for gen in list(gens):
-            try:
-                next(gen)
-            except StopIteration:
-                gens.remove(gen)
+HOP = 3.0
+GAP = 8.0
+FLOW = 8.0
+WORK = 0.9
+GROUPS = ((0, 1, 2),)
 
 
 def kernel(
@@ -88,6 +85,13 @@
     tok = 2 * nz * ny
     units = nz * ny
     hid = tok * rows
+    pieces = [(h, ms) for h in range(heads) for ms in GROUPS]
+    gather_order = [
+        p for h in range(heads)
+        for p in sorted(
+            (p for p in range(len(pieces)) if pieces[p][0] == h), key=lambda p: pieces[p][1]
+        )
+    ]
 
     me = lax.axis_index("tok")
     c = lax.rem(me, 2)
@@ -134,31 +138,32 @@
         jnp.where(z < nz - 1, 1, 0) + jnp.where(z > 0, 1, 0) + (2 if ny > 1 else 1),
     )
 
-    def ag_copy(s, h, slot, way):
+    def ag_copy(s, p, slot, way):
         dev = (up, down, across, sib)[way]
-        ref = wg.at[s, h, slot]
-        return rdma(ref, ref, ag_ssem.at[s, h, way, slot], ag_rsem.at[s, h, slot], dev)
-
-    def ag_start(s, h):
-        pl.when(z < nz - 1)(lambda: ag_copy(s, h, me, 0).start())
-        pl.when(z > 0)(lambda: ag_copy(s, h, me, 1).start())
+        h, ms = pieces[p]
+        ref = wg.at[s, h, slot, pl.ds(ms[0], len(ms))]
+        return rdma(ref, ref, ag_ssem.at[s, p, way, slot], ag_rsem.at[s, p, slot], dev)
+
+    def ag_start(s, p):
+        pl.when(z < nz - 1)(lambda: ag_copy(s, p, me, 0).start())
+        pl.when(z > 0)(lambda: ag_copy(s, p, me, 1).start())
         if ny > 1:
-            ag_copy(s, h, me, 2).start()
-        ag_copy(s, h, me, 3).start()
-
-    def ag_steps(s, h):
+            ag_copy(s, p, me, 2).start()
+        ag_copy(s, p, me, 3).start()
+
+    def ag_steps(s, p):
         def from_z(slot, way):
-            ag_copy(s, h, slot, way).wait_recv()
+            ag_copy(s, p, slot, way).wait_recv()
             pl.when((z < nz - 1) if way == 0 else (z > 0))(
-                lambda: ag_copy(s, h, slot, way).start()
+                lambda: ag_copy(s, p, slot, way).start()
             )
             if ny > 1:
-                ag_copy(s, h, slot, 2).start()
-            ag_copy(s, h, slot, 3).start()
+                ag_copy(s, p, slot, 2).start()
+            ag_copy(s, p, slot, 3).start()
 
         def from_y(slot):
-            ag_copy(s, h, slot, 3).wait_recv()
-            ag_copy(s, h, slot, 3).start()
+            ag_copy(s, p, slot, 3).wait_recv()
+            ag_copy(s, p, slot, 3).start()
 
         for j in range(1, nz + 1):
             if j < nz:
@@ -173,17 +178,17 @@
                     pl.when(z + d < nz)(lambda: from_y(at(z + d, 1 - y, c)))
             yield
         for u in range(units):
-            ag_copy(s, h, u * 2 + 1 - c, 3).wait_recv()
-
-    def ag_drain(s, h):
+            ag_copy(s, p, u * 2 + 1 - c, 3).wait_recv()
+
+    def ag_drain(s, p):
         for zz in range(nz):
             slot = at(zz, y, c)
-            pl.when((zz <= z) & (z < nz - 1))(lambda: ag_copy(s, h, slot, 0).wait_send())
-            pl.when((zz >= z) & (z > 0))(lambda: ag_copy(s, h, slot, 1).wait_send())
-            if ny > 1:
-                ag_copy(s, h, slot, 2).wait_send()
+            pl.when((zz <= z) & (z < nz - 1))(lambda: ag_copy(s, p, slot, 0).wait_send())
+            pl.when((zz >= z) & (z > 0))(lambda: ag_copy(s, p, slot, 1).wait_send())
+            if ny > 1:
+                ag_copy(s, p, slot, 2).wait_send()
             for yy in range(ny):
-                ag_copy(s, h, at(zz, yy, c), 3).wait_send()
+                ag_copy(s, p, at(zz, yy, c), 3).wait_send()
 
     def weight(s, h, m):
         return wg[s, h, :, m].reshape(hid, dh)
@@ -234,29 +239,34 @@
         out_ref[s, :, cols(h)] = (raw * scale).astype(BF16)
         yield
 
-    def y_copy(s, h, zd):
+    def y_copy(s, p, zd):
+        h, ms = pieces[p]
+        part_of = pl.ds(ms[0], len(ms))
         return rdma(
-            ysend.at[s, h, zd], yrecv.at[s, h, zd],
-            y_ssem.at[s, h, zd], y_rsem.at[s, h, zd], across,
-        )
-
-    def z_copy(s, h, zd, way):
+            ysend.at[s, h, zd, part_of], yrecv.at[s, h, zd, part_of],
+            y_ssem.at[s, p, zd], y_rsem.at[s, p, zd], across,
+        )
+
+    def z_copy(s, p, zd, way):
+        h, ms = pieces[p]
+        part_of = pl.ds(ms[0], len(ms))
         return rdma(
-            zsend.at[s, h, zd], zrecv.at[s, h, way, zd],
-            z_ssem.at[s, h, zd], z_rsem.at[s, h, way, zd], (up, down)[way],
+            zsend.at[s, h, zd, part_of], zrecv.at[s, h, way, zd, part_of],
+            z_ssem.at[s, p, zd], z_rsem.at[s, p, way, zd], (up, down)[way],
         )
 
     def pair(s, h, m, u):
         return part[s, h, m, c, u].astype(F32) + sibrecv[s, h, m, u].astype(F32)
 
-    def rs_steps(s, h):
-        for m in (2, 0, 1):
+    def rs_steps(s, p):
+        h, ms = pieces[p]
+        for m in ms:
             sib_copy(s, h, m).wait_recv()
 
         def send_y(zd):
-            for m in range(3):
+            for m in ms:
                 ysend[s, h, zd, m] = pair(s, h, m, zd * ny + 1 - y).astype(BF16)
-            y_copy(s, h, zd).start()
+            y_copy(s, p, zd).start()
 
         if ny > 1:
             for d in range(nz - 1, 0, -1):
@@ -274,63 +284,63 @@
         def send_z(zd, way):
             more = (z > 0) if way == 0 else (z < nz - 1)
             if ny > 1:
-                y_copy(s, h, zd).wait_recv()
+                y_copy(s, p, zd).wait_recv()
 
             @pl.when(more)
             def _():
-                z_copy(s, h, zd, way).wait_recv()
-                for m in range(3):
+                z_copy(s, p, zd, way).wait_recv()
+                for m in ms:
                     zsend[s, h, zd, m] = (
                         quad(zd, m) + zrecv[s, h, way, zd, m].astype(F32)
                     ).astype(BF16)
 
             @pl.when(jnp.logical_not(more))
             def _():
-                for m in range(3):
+                for m in ms:
                     zsend[s, h, zd, m] = quad(zd, m).astype(BF16)
 
-            z_copy(s, h, zd, way).start()
+            z_copy(s, p, zd, way).start()
 
         for d in range(nz - 1, 0, -1):
             pl.when(z + d < nz)(lambda: send_z(z + d, 0))
             pl.when(z - d >= 0)(lambda: send_z(z - d, 1))
             yield
         if ny > 1:
-            y_copy(s, h, z).wait_recv()
-        for m in range(3):
+            y_copy(s, p, z).wait_recv()
+        for m in ms:
             acc[m] = quad(z, m)
 
         def add(way):
-            z_copy(s, h, z, way).wait_recv()
-            for m in range(3):
+            z_copy(s, p, z, way).wait_recv()
+            for m in ms:
                 acc[m] = acc[m] + zrecv[s, h, way, z, m].astype(F32)
 
         pl.when(z > 0)(lambda: add(0))
         pl.when(z < nz - 1)(lambda: add(1))
-        old = cur[h]
-        new = renorm(old, old + acc[...])
+        for m in ms:
+            old = cur[h, m]
+            new = renorm(old, old + acc[m])
+            if s + 1 < spans:
+                cur[h, m] = new
+                wg[s + 1, h, me, m] = new.astype(BF16)
+            else:
+                fin_ref[h, m] = new
         if s + 1 < spans:
-            cur[h] = new
-            wg[s + 1, h, me] = new.astype(BF16)
-            ag_start(s + 1, h)
-        else:
-            fin_ref[h] = new
-
-    def rs_drain(s, h):
-        for m in range(3):
+            ag_start(s + 1, p)
+        yield
+
+    def rs_drain(s, p):
+        h, ms = pieces[p]
+        for m in ms:
             sib_copy(s, h, m).wait_send()
         for zd in range(nz):
             if ny > 1:
-                y_copy(s, h, zd).wait_send()
-            pl.when(zd > z)(lambda: z_copy(s, h, zd, 0).wait_send())
-            pl.when(zd < z)(lambda: z_copy(s, h, zd, 1).wait_send())
-
-    def then(*gens):
-        for gen in gens:
-            yield from gen
-
-    for h in range(heads):
-        ag_start(0, h)
+                y_copy(s, p, zd).wait_send()
+            pl.when(zd > z)(lambda: z_copy(s, p, zd, 0).wait_send())
+            pl.when(zd < z)(lambda: z_copy(s, p, zd, 1).wait_send())
+
+    for p in gather_order:
+        ag_start(0, p)
     loads[0].wait()
     loads[1].wait()
     for s in range(spans):
@@ -338,24 +348,46 @@
             vt_ref[s, h] = v_ref[s, :, cols(h)].T
     loads[2].wait()
 
+    tasks = []
+
+    def plan(gen, times):
+        for time in times:
+            tasks.append((time, len(tasks), gen))
+        return times[-1]
+
+    def until(start, end=0.0):
+        return [start + HOP * j for j in range(1, nz + 1)] + [start + HOP * nz + 1.0 + end]
+
+    ready = {}
+    for i, p in enumerate(gather_order):
+        ready[p] = plan(ag_steps(0, p), until(GAP * i))
+    busy = 0.0
     for s in range(spans):
-        if s == 0:
-            merge(ag_steps(s, 0))
+        link = 0.0
+        fresh = {}
         for h in range(heads):
-            others = []
-            if h + 1 < heads:
-                others.append(ag_steps(s, h + 1))
-            if h > 0:
-                others.append(rs_steps(s, h - 1))
-            merge(kv_steps(s, h), *others)
-        last = [rs_steps(s, heads - 1)]
-        if s + 1 < spans:
-            last.append(ag_steps(s + 1, 0))
-        merge(then(*[q_steps(s, h) for h in range(heads)]), *last)
+            own = [p for p in range(len(pieces)) if pieces[p][0] == h]
+            begin = max(busy, max(ready[p] for p in own)) + 0.1
+            stages = [begin + WORK * j for j in range(4)]
+            busy = plan(kv_steps(s, h), stages)
+            for p in own:
+                given = max(stages[{2: 1, 0: 2, 1: 3}[m]] for m in pieces[p][1])
+                link = max(given + 1.5, link)
+                rs = [link] + [link + HOP * j for j in range(1, nz + 1)]
+                end = plan(rs_steps(s, p), rs)
+                if s + 1 < spans:
+                    fresh[p] = plan(ag_steps(s + 1, p), until(end))
+                link += FLOW if s + 1 < spans else GAP
+        for h in range(heads):
+            start = busy + 1.6 + h * 4.0
+            plan(q_steps(s, h), [start, start + 2.0])
+        ready = fresh
+    for _, _, gen in sorted(tasks, key=lambda task: task[:2]):
+        next(gen, None)
     for s in range(spans):
-        for h in range(heads):
-            ag_drain(s, h)
-            rs_drain(s, h)
+        for p in range(len(pieces)):
+            ag_drain(s, p)
+            rs_drain(s, p)
 
 
 def fused_on_device(nz, ny, queries, keys, values, rates, fast_weights):
@@ -365,6 +397,7 @@
     units = nz * ny
     unit = (three, rows, dh)
     sh = (spans, heads)
+    sp = (spans, heads * len(GROUPS))
     vmem = pl.BlockSpec(memory_space=pltpu.VMEM)
     hbm = pl.BlockSpec(memory_space=pl.ANY)
     dma = pltpu.SemaphoreType.DMA
@@ -392,14 +425,14 @@
             pltpu.VMEM(sh + (2, nz) + unit, BF16),
             pltpu.VMEM(unit, F32),
             dma((3,)),
-            dma(sh + (4, tok)),
-            dma(sh + (tok,)),
+            dma(sp + (4, tok)),
+            dma(sp + (tok,)),
             dma(sh + (three,)),
             dma(sh + (three,)),
-            dma(sh + (nz,)),
-            dma(sh + (nz,)),
-            dma(sh + (nz,)),
-            dma(sh + (2, nz)),
+            dma(sp + (nz,)),
+            dma(sp + (nz,)),
+            dma(sp + (nz,)),
+            dma(sp + (2, nz)),
         ],
         compiler_params=pltpu.CompilerParams(
             collective_id=0, has_side_effects=True, vmem_limit_bytes=56 * 1024 * 1024

time: 130 us -> 101 us (0.78)
  Pallas kernels: 126 us -> 97.3 us
    pallas_call x1, Pallas kernels: 126 us -> 97.3 us  [fused_on_device(): pl.pallas_call(functools.partial(kernel, nz, ny), out_shape=(jax.ShapeDty...]
where the time goes in v2:
time: 101 us
  Pallas kernels  97.3 us (96%)
  local copies, waits for them, and re-layouts  3.06 us (3%)
    pallas_call x1, Pallas kernels, fused_on_device(): pl.pallas_call(functools.partial(kernel, nz, ny), out_shape=(jax.ShapeDty...  97.3 us
    unnamed x4, local copies, waits for them, and re-layouts  3.06 us

profile of v2, /device:TPU:0, one launch (start us, length us, event | category | flops | bytes accessed | tf_op | source)
XLA Modules:
  0.0 101.0 jit_solution(16309579856427373198)
XLA Ops:
  0.6 97.3 %shard_map.68 = (bf16[2,256,1024]{2,1,0:T(8,128)(2,1)}, f32[2,3,32,512]{3,2,1,0:T(8,128)}) custom-call(bf16[2,256,1024]{2,1,0:T(8,128)(2,1)} %q_hbm.1, bf16[2,256,1024]{2,1,0:T(8,128)(2,1)} %k_hbm.1, bf16[2,256,1024]{2,1,0:T(8,128)(2,1)} %v_hbm.1, f32[2,3,2,256]{3,2,1,0:T(2,128)} %rates_ref.1, f32[2,3,32,512]{3,2,1,0:T(8,128)} %w_ref.1), custom_call_target="tpu_custom_call" | custom-call | flops 4831838208 | bytes 4194304 | tf_op jit(solution)/shard_map/pallas_call | solution.py:405
  98.0 0.0 copy-start
  98.0 2.3 %copy.9 = bf16[2,256,1024]{2,1,0:T(8,128)(2,1)} copy(bf16[2,256,1024]{2,1,0:T(8,128)(2,1)} %get-tuple-element.4) | data formatting | bytes 2097152
  100.3 0.0 copy-done
  100.3 0.7 copy.10
Async XLA Ops:
  98.0 2.3 %copy-start = (f32[2,3,32,512]{3,2,1,0:T(8,128)S(1)}, f32[2,3,32,512]{3,2,1,0:T(8,128)}, u32[]{:S(2)}) copy-start(f32[2,3,32,512]{3,2,1,0:T(8,128)} %get-tuple-element.5) | copy-start | bytes 1179652
